TPU v7x, 256 devices: a whole 4x4x8 slice. The times are simulated.
256 devices in a mesh: dom: 64 (over y, z, core), kv: 4 (over x).
Axes of the slice: x: 4, y: 4, z: 8, core: 2. Of those that a mesh axis runs over, the one named last changes fastest.
Arguments:
- node_feats: bfloat16 [32768, 128], P(('dom', 'kv')), may hold values from -11 to 11
- positions: float32 [3, 32768], P(None, ('dom', 'kv')), may hold values from 0 to 2304, as said below
- species: int32 [32768], P(('dom', 'kv')), may hold values from 0 to 1
- halo_rows: int32 [256, 64], P(('dom', 'kv')), may hold values from 0 to 127, as said below
- neighbours: int32 [32768, 32], P(('dom', 'kv')), may hold values from 0 to 191, as said below
- nbr_count: int32 [32768], P(('dom', 'kv')), may hold values from 16 to 32, as said below
- recip_vectors: int32 [3, 16384], replicated, may hold values from -13 to 13, as said below
- w_msg: bfloat16 [128, 128], replicated, may hold values from -0.5 to 0.5
- w_rad1: bfloat16 [8, 128], replicated, may hold values from -2 to 2
- w_rad2: bfloat16 [128, 256], replicated, may hold values from -0.5 to 0.5
- w_upd: bfloat16 [384, 128], replicated, may hold values from -0.3125 to 0.3125
- w_out: bfloat16 [128], replicated, may hold values from -0.5 to 0.5
- chi_table: float32 [2], replicated, may hold values from -1 to 1
- hard_table: float32 [2], replicated, may hold values from 0.5 to 2
Outputs:
- electroneg: float32 [32768], P(('dom', 'kv'))
- charges: float32 [32768], P(('dom', 'kv'))
Inputs may be any that keep to these rules, and one draw needn't show every extreme that they name: `halo_rows`: in each slab's row, 64 distinct local atom indices; the first 32 lie near the slab's lower face, the rest near its upper face. `neighbours`: an atom never lists its own local index. `nbr_count`: the first atom of every slab has all 32 slots live. `recip_vectors`: distinct nonzero triples. `positions`: atoms of slab s have first coordinate in [9 s, 9 (s + 1)), the other two in [0, 20).
All inputs are finite; a program needn't handle non-finite values.
Results may differ from a plain program's by a relative error of at most 0.003.
Values may be sent and summed in bfloat16 or wider, within the bound.
A program may use at most 128 MiB of HBM per device.

v0:
```python
import math
import jax
import jax.numpy as jnp
from jax import lax
from jax.sharding import PartitionSpec as P

ITERS = 4
slab_width = 9.0
side_length = 20.0
two_pi = 2.0 * math.pi
highest = lax.Precision.HIGHEST


def with_halo(block, sides, width):
    for axis, dim in sides:
        count = lax.axis_size(axis)
        forward = [(i, i + 1) for i in range(count - 1)]
        forward.append((count - 1, 0))
        backward = [(target, source) for source, target in forward]
        low = lax.ppermute(
            lax.slice_in_dim(block, block.shape[dim] - width, None, axis=dim), axis, forward
        )
        high = lax.ppermute(lax.slice_in_dim(block, 0, width, axis=dim), axis, backward)
        block = jnp.concatenate([low, block, high], axis=dim)
    return block


def wrapped(offset, length):
    return jnp.where(
        offset > 0.5 * length,
        offset - length,
        jnp.where(offset < -0.5 * length, offset + length, offset),
    )


def recip_setup(coords, triples, box_x, atoms_total):
    comp_x = triples[0].astype(jnp.float32)
    comp_y = triples[1].astype(jnp.float32)
    comp_z = triples[2].astype(jnp.float32)
    phase_arg = two_pi * (
        coords[0][:, None] * (comp_x / box_x)[None, :]
        + coords[1][:, None] * (comp_y / side_length)[None, :]
        + coords[2][:, None] * (comp_z / side_length)[None, :]
    )
    phase_table = jnp.concatenate([jnp.cos(phase_arg), jnp.sin(phase_arg)], axis=1)
    m_square = comp_x * comp_x + comp_y * comp_y + comp_z * comp_z
    weight = 16.0 / atoms_total * jnp.exp(-m_square / 400.0) / (1.0 + m_square / 16.0)
    return (phase_table, weight)


def message_layer(
    ext_proj,
    ext_pos,
    own_pos,
    own_feats,
    nbr_index,
    counts,
    kinds,
    w_rad1,
    w_rad2,
    w_upd,
    w_out,
    chi_table,
    box_x,
):
    atoms_dev, slot_count = nbr_index.shape
    channels = own_feats.shape[1]
    flat_index = nbr_index.reshape(-1)
    nbr_proj = jnp.take(ext_proj, flat_index, axis=0).reshape(atoms_dev, slot_count, channels)
    nbr_pos = jnp.take(ext_pos, flat_index, axis=1).reshape(3, atoms_dev, slot_count)
    displace = jnp.stack(
        [
            wrapped(nbr_pos[0] - own_pos[0][:, None], box_x),
            wrapped(nbr_pos[1] - own_pos[1][:, None], side_length),
            wrapped(nbr_pos[2] - own_pos[2][:, None], side_length),
        ]
    )
    distance = jnp.sqrt(jnp.sum(displace * displace, axis=0) + 0.25)
    unit_vec = displace / distance
    basis_count = w_rad1.shape[0]
    centres = 1.0 + 1.25 * jnp.arange(basis_count, dtype=jnp.float32)
    radial_basis = jnp.exp(-jnp.square((distance[:, :, None] - centres) / 1.25)).astype(
        jnp.bfloat16
    )
    hidden = jax.nn.silu(
        jnp.dot(radial_basis.reshape(-1, basis_count), w_rad1, preferred_element_type=jnp.float32)
    ).astype(jnp.bfloat16)
    radial = jnp.dot(hidden, w_rad2, preferred_element_type=jnp.float32).reshape(
        atoms_dev, slot_count, 2 * channels
    )
    live_mask = (jnp.arange(slot_count)[None, :] < counts[:, None]).astype(jnp.float32)
    radial = radial * live_mask[:, :, None]
    msg_scale = 1.0 / math.sqrt(slot_count)
    scalar_msg = jnp.sum(radial[:, :, :channels] * nbr_proj, axis=1) * msg_scale
    carried = radial[:, :, channels:] * nbr_proj
    vector_msg = jnp.sum(unit_vec[:, :, :, None] * carried[None], axis=2) * msg_scale
    vec_square = jnp.sum(vector_msg * vector_msg, axis=0)
    joined = jnp.concatenate(
        [scalar_msg, vec_square, own_feats.astype(jnp.float32)], axis=1
    ).astype(jnp.bfloat16)
    update = jax.nn.silu(jnp.dot(joined, w_upd, preferred_element_type=jnp.float32)).astype(
        jnp.bfloat16
    )
    one_hot = (kinds[:, None] == jnp.arange(chi_table.shape[0])[None, :]).astype(jnp.float32)
    return jnp.dot(update, w_out, preferred_element_type=jnp.float32) + jnp.sum(
        one_hot * chi_table[None, :], axis=1
    )


def squares(residual):
    return lax.psum(jnp.sum(residual * residual, axis=1), ("dom", "kv"))


def local(
    node_feats,
    positions,
    species,
    halo_rows,
    neighbours,
    nbr_count,
    recip_vectors,
    w_msg,
    w_rad1,
    w_rad2,
    w_upd,
    w_out,
    chi_table,
    hard_table,
):
    atoms_dev = node_feats.shape[0]
    halo_width = halo_rows.shape[1] // 2
    slab_count = lax.axis_size("dom") * lax.axis_size("kv")
    box_x = slab_count * slab_width
    atoms_total = atoms_dev * slab_count
    send_rows = halo_rows[0]
    packet_feats = jnp.take(node_feats, send_rows, axis=0)
    packet_pos = jnp.take(positions, send_rows, axis=1).T
    got_feats = with_halo(packet_feats, ((("dom", "kv"), 0),), halo_width)
    got_pos = with_halo(packet_pos, ((("dom", "kv"), 0),), halo_width)
    own_proj = jnp.dot(node_feats, w_msg, preferred_element_type=jnp.float32).astype(jnp.bfloat16)
    far_feats = jnp.concatenate([got_feats[:halo_width], got_feats[3 * halo_width :]], axis=0)
    far_proj = jnp.dot(far_feats, w_msg, preferred_element_type=jnp.float32).astype(jnp.bfloat16)
    ext_proj = jnp.concatenate([own_proj, far_proj], axis=0)
    ext_pos = jnp.concatenate(
        [positions, got_pos[:halo_width].T, got_pos[3 * halo_width :].T], axis=1
    )
    electroneg = message_layer(
        ext_proj,
        ext_pos,
        positions,
        node_feats,
        neighbours,
        nbr_count,
        species,
        w_rad1,
        w_rad2,
        w_upd,
        w_out,
        chi_table,
        box_x,
    )
    one_hot = (species[:, None] == jnp.arange(hard_table.shape[0])[None, :]).astype(jnp.float32)
    hardness = jnp.sum(one_hot * hard_table[None, :], axis=1)
    phase_table, weight = recip_setup(positions, recip_vectors, box_x, atoms_total)
    weight_pair = jnp.concatenate([weight, weight])
    right_side = jnp.stack([-electroneg, jnp.ones_like(electroneg)])
    solution = jnp.zeros_like(right_side)
    residual = right_side
    direction = right_side
    norm_now = squares(residual)
    for iteration in range(ITERS):
        partial_value = jnp.dot(
            direction, phase_table, precision=highest, preferred_element_type=jnp.float32
        )
        summed = lax.psum(partial_value, ("dom", "kv"))
        potential = lax.dot_general(
            summed * weight_pair,
            phase_table,
            (((1,), (1,)), ((), ())),
            precision=highest,
            preferred_element_type=jnp.float32,
        )
        applied = hardness * direction + potential
        curvature = lax.psum(jnp.sum(direction * applied, axis=1), ("dom", "kv"))
        step_size = norm_now / curvature
        solution = solution + step_size[:, None] * direction
        residual = residual - step_size[:, None] * applied
        if iteration + 1 < ITERS:
            norm_next = squares(residual)
            direction = residual + (norm_next / norm_now)[:, None] * direction
            norm_now = norm_next
    totals = lax.psum(jnp.sum(solution, axis=1), ("dom", "kv"))
    charges = solution[0] - totals[0] / totals[1] * solution[1]
    return (electroneg, charges)


def solution(mesh):
    return jax.shard_map(
        local,
        mesh=mesh,
        in_specs=(
            P(("dom", "kv"), None),
            P(None, ("dom", "kv")),
            P(("dom", "kv")),
            P(("dom", "kv"), None),
            P(("dom", "kv"), None),
            P(("dom", "kv")),
            P(),
            P(),
            P(),
            P(),
            P(),
            P(),
            P(),
            P(),
        ),
        out_specs=(P(("dom", "kv")), P(("dom", "kv"))),
        check_vma=False,
    )
```

profile of v0, /device:TPU:1, one launch (start us, length us, event | category | flops | bytes accessed | tf_op | source)
XLA Modules:
  0.0 1828.8 jit_solution(18002408356740054125)
XLA Ops:
  10.0 2.1 collective-permute-start.2
  12.1 1.9 collective-permute-start.3
  15.6 3.1 collective-permute-start.1
  25.4 33.0 %fusion.1 = (f32[128,16384]{1,0:T(8,128)}, f32[128,16384]{1,0:T(8,128)}) fusion(f32[16384]{0:T(1024)S(1)} %bitcast.46, f32[128]{0:T(128)S(1)} %get-tuple-element.32, f32[16384]{0:T(1024)S(1)} %bitcast.47, f32[128]{0:T(128)S(1)} %get-tuple-element.33, f32[16384]{0:T(1024)S(1)} %bitcast.45, f32[128]{0:T(128)S(1)} %get-tuple-element.31), kind=kLoop, calls=%fused_computation.7 | loop fusion | flops 12582912 | bytes 16975360 | tf_op jit(solution)/shard_map/cos | solution.py:45
  58.5 10.8 gather_fusion.1
  69.3 2.1 select_bitcast_fusion
  71.5 2.8 slice_reduce_fusion.2
  75.2 3.3 fusion.3
  78.5 3.9 broadcast_multiply_fusion
  82.7 12.1 gather_fusion.3
  94.9 3.3 fusion.2
  98.2 2.2 multiply_reduce_fusion
  100.8 13.9 fusion.41
  114.8 253.6 %all-reduce.7.cloned.1.call-done = f32[2,32768]{1,0:T(2,128)} async-done(((f32[2,32768]{1,0:T(2,128)}), f32[2,32768]{1,0:T(2,128)}) %all-reduce.7.cloned.1.call-update) | async-done | bytes 262160 | tf_op jit(solution)/shard_map/psum | solution.py:175
  368.4 16.8 fusion.44
  385.2 77.9 %all-reduce.1 = (f32[2]{0:T(128)S(1)}, f32[2]{0:T(128)S(1)}) all-reduce(f32[2]{0:T(128)S(1)} %get-tuple-element.6, f32[2]{0:T(128)S(1)} %get-tuple-element.5), channel_id=1, replica_groups=mesh['dom'=64,'kv'=4] {'dom','kv'}, use_global_device_ids=true, to_apply=%region_6.7 | all-reduce | flops 4 | bytes 32 | tf_op jit(solution)/shard_map/psum | solution.py:111
  463.2 73.2 %psum.94 = f32[2]{0:T(128)S(1)} all-reduce(f32[2]{0:T(128)S(1)} %get-tuple-element.17), channel_id=1, replica_groups=mesh['dom'=64,'kv'=4] {'dom','kv'}, use_global_device_ids=true, to_apply=%region_12.13 | all-reduce | flops 2 | bytes 16 | tf_op jit(solution)/shard_map/psum | solution.py:111
  536.5 13.6 fusion.61
  550.2 245.8 %all-reduce.9.cloned.1.call-done = f32[2,32768]{1,0:T(2,128)} async-done(((f32[2,32768]{1,0:T(2,128)}), f32[2,32768]{1,0:T(2,128)}) %all-reduce.9.cloned.1.call-update) | async-done | bytes 262160 | tf_op jit(solution)/shard_map/psum | solution.py:175
  796.0 16.9 multiply_reduce_fusion.6
  812.9 77.4 %psum.96 = f32[2]{0:T(128)S(1)} all-reduce(f32[2]{0:T(128)S(1)} %get-tuple-element.37), channel_id=1, replica_groups=mesh['dom'=64,'kv'=4] {'dom','kv'}, use_global_device_ids=true, to_apply=%region_15.16 | all-reduce | flops 2 | bytes 16 | tf_op jit(solution)/shard_map/psum | solution.py:184
  890.5 73.4 %psum.97 = f32[2]{0:T(128)S(1)} all-reduce(f32[2]{0:T(128)S(1)} %get-tuple-element.15), channel_id=1, replica_groups=mesh['dom'=64,'kv'=4] {'dom','kv'}, use_global_device_ids=true, to_apply=%region_17.18 | all-reduce | flops 2 | bytes 16 | tf_op jit(solution)/shard_map/psum | solution.py:111
  964.1 13.6 fusion.60
  977.7 245.9 %all-reduce.11.cloned.1.call-done = f32[2,32768]{1,0:T(2,128)} async-done(((f32[2,32768]{1,0:T(2,128)}), f32[2,32768]{1,0:T(2,128)}) %all-reduce.11.cloned.1.call-update) | async-done | bytes 262160 | tf_op jit(solution)/shard_map/psum | solution.py:175
  1223.7 17.0 multiply_reduce_fusion.4
  1240.7 77.4 %psum.99 = f32[2]{0:T(128)S(1)} all-reduce(f32[2]{0:T(128)S(1)} %get-tuple-element.39), channel_id=1, replica_groups=mesh['dom'=64,'kv'=4] {'dom','kv'}, use_global_device_ids=true, to_apply=%region_20.21 | all-reduce | flops 2 | bytes 16 | tf_op jit(solution)/shard_map/psum | solution.py:184
  1318.3 73.5 %psum.100 = f32[2]{0:T(128)S(1)} all-reduce(f32[2]{0:T(128)S(1)} %get-tuple-element.13), channel_id=1, replica_groups=mesh['dom'=64,'kv'=4] {'dom','kv'}, use_global_device_ids=true, to_apply=%region_22.23 | all-reduce | flops 2 | bytes 16 | tf_op jit(solution)/shard_map/psum | solution.py:111
  1391.8 13.6 fusion.59
  1405.4 245.9 %all-reduce.13.cloned.1.call-done = f32[2,32768]{1,0:T(2,128)} async-done(((f32[2,32768]{1,0:T(2,128)}), f32[2,32768]{1,0:T(2,128)}) %all-reduce.13.cloned.1.call-update) | async-done | bytes 262160 | tf_op jit(solution)/shard_map/psum | solution.py:175
  1651.3 17.1 fusion.5
  1668.4 77.4 %psum.102 = f32[2]{0:T(128)S(1)} all-reduce(f32[2]{0:T(128)S(1)} %fusion.5), channel_id=1, replica_groups=mesh['dom'=64,'kv'=4] {'dom','kv'}, use_global_device_ids=true, to_apply=%region_25.26 | all-reduce | flops 2 | bytes 16 | tf_op jit(solution)/shard_map/psum | solution.py:184
  1746.0 73.2 %psum.103 = f32[2]{0:T(128)S(1)} all-reduce(f32[2]{0:T(128)S(1)} %get-tuple-element.11), channel_id=1, replica_groups=mesh['dom'=64,'kv'=4] {'dom','kv'}, use_global_device_ids=true, to_apply=%region_27.28 | all-reduce | flops 2 | bytes 16 | tf_op jit(solution)/shard_map/psum | solution.py:192
  (87 shorter events, 14.7 us)
Async XLA Ops:
  7.2 93.3 %copy-start = (bf16[384,128]{1,0:T(8,128)(2,1)S(1)}, bf16[384,128]{1,0:T(8,128)(2,1)}, u32[]{:S(2)}) copy-start(bf16[384,128]{1,0:T(8,128)(2,1)} %param.24) | copy-start | bytes 294916
  7.2 361.2 %all-reduce.7.cloned.1.call-start = ((), (), s32[]{:S(2)}) async-start(), calls=%async_computation | async-start | bytes 524288 | tf_op jit(solution)/shard_map/psum | solution.py:175
  10.0 72.5 %collective-permute-start.2 = (bf16[32,128]{1,0:T(8,128)(2,1)S(1)}, bf16[32,128]{1,0:T(8,128)(2,1)S(1)}, u32[]{:S(2)}, u32[]{:S(2)}) collective-permute-start(bf16[32,128]{1,0:T(8,128)(2,1)S(1)} %get-tuple-element.29), channel_id=1, source_target_pairs={{0,1},{1,2},{2,3},{3,4},{4,5},{5,6},{6,7},{7,8},{8,9},{9,10},{10,1... | collective-permute-start | bytes 24584 | tf_op jit(solution)/shard_map/ppermute | solution.py:20
  12.1 70.4 %collective-permute-start.3 = (bf16[32,128]{1,0:T(8,128)(2,1)S(1)}, bf16[32,128]{1,0:T(8,128)(2,1)S(1)}, u32[]{:S(2)}, u32[]{:S(2)}) collective-permute-start(bf16[32,128]{1,0:T(8,128)(2,1)S(1)} %get-tuple-element.30), channel_id=1, source_target_pairs={{1,0},{2,1},{3,2},{4,3},{5,4},{6,5},{7,6},{8,7},{9,8},{10,9},{11,1... | collective-permute-start | bytes 24584 | tf_op jit(solution)/shard_map/ppermute | solution.py:23
  15.5 43.0 %collective-permute-start = (f32[32,3]{1,0:T(8,128)S(1)}, f32[32,3]{1,0:T(8,128)S(1)}, u32[]{:S(2)}, u32[]{:S(2)}) collective-permute-start(f32[32,3]{1,0:T(8,128)S(1)} %get-tuple-element.27), channel_id=1, source_target_pairs={{0,1},{1,2},{2,3},{3,4},{4,5},{5,6},{6,7},{7,8},{8,9},{9,10},{10,1... | collective-permute-start | bytes 1160 | tf_op jit(solution)/shard_map/ppermute | solution.py:20
  15.6 42.9 %collective-permute-start.1 = (f32[32,3]{1,0:T(8,128)S(1)}, f32[32,3]{1,0:T(8,128)S(1)}, u32[]{:S(2)}, u32[]{:S(2)}) collective-permute-start(f32[32,3]{1,0:T(8,128)S(1)} %get-tuple-element.28), channel_id=1, source_target_pairs={{1,0},{2,1},{3,2},{4,3},{5,4},{6,5},{7,6},{8,7},{9,8},{10,9},{11,1... | collective-permute-start | bytes 1160 | tf_op jit(solution)/shard_map/ppermute | solution.py:23
  58.4 16.8 copy-start.3
  58.4 16.8 copy-start.4
  75.2 7.4 copy-start.2
  82.7 17.8 copy-start.1
  82.7 17.8 copy-start.5
  100.8 13.9 copy-start.6
  114.7 681.3 %all-reduce.9.cloned.1.call-start = ((), (), s32[]{:S(2)}) async-start(), calls=%async_computation.1 | async-start | bytes 524288 | tf_op jit(solution)/shard_map/psum | solution.py:175
  550.1 673.5 %all-reduce.11.cloned.1.call-start = ((), (), s32[]{:S(2)}) async-start(), calls=%async_computation.2 | async-start | bytes 524288 | tf_op jit(solution)/shard_map/psum | solution.py:175
  977.7 673.6 %all-reduce.13.cloned.1.call-start = ((), (), s32[]{:S(2)}) async-start(), calls=%async_computation.3 | async-start | bytes 524288 | tf_op jit(solution)/shard_map/psum | solution.py:175
Sparse Core Ops, SparseCore 0:
  114.9 253.4 all-reduce.6
  550.2 245.7 all-reduce.8
  977.8 245.8 all-reduce.10
  1405.6 245.7 all-reduce.12
where the time goes:
time: 1830 us
  waiting for transfers between devices  991 us (54%)
  blocking collectives  604 us (33%)
  matrix products  127 us (7%)
  other arithmetic  51.7 us (3%)
  local copies, waits for them, and re-layouts  31.7 us (2%)
    psum x4, waiting for transfers between devices, local(): summed = lax.psum(partial_value, ('dom', 'kv'))  991 us
    psum x4, blocking collectives, squares(): return lax.psum(jnp.sum(residual * residual, axis=1), ('dom', 'kv'))  298 us
    psum x3, blocking collectives, local(): curvature = lax.psum(jnp.sum(direction * applied, axis=1), ('dom', 'kv'))  232 us
    psum x1, blocking collectives, local(): totals = lax.psum(jnp.sum(solution, axis=1), ('dom', 'kv'))  73.2 us
    dot_general x4, matrix products, local(): lax.dot_general(summed * weight_pair, phase_table, (((1,), (1,)), ((), ()...  67.8 us
    dot_general x4, matrix products, local(): jnp.dot(direction, phase_table, precision=highest, preferred_element_type...  54.7 us
  transfers between devices with their start and end apart: 8, of which 4 were waited for; matrix products, arithmetic and copies ran while one was open for 4% of the time, Pallas kernels for 0%

commit v1 on v0

--- a/solution.py
+++ b/solution.py
@@ -189,7 +189,9 @@
             norm_next = squares(residual)
             direction = residual + (norm_next / norm_now)[:, None] * direction
             norm_now = norm_next
-    totals = lax.psum(jnp.sum(solution, axis=1), ("dom", "kv"))
+    totals = jnp.sum(solution, axis=1)
+    for name in ("kv", "dom"):
+        totals = lax.psum(totals, name)
     charges = solution[0] - totals[0] / totals[1] * solution[1]
     return (electroneg, charges)
 

time: 1830 us -> 1890 us (1.033)
  blocking collectives: 604 us -> 664 us
    psum x1 -> x2, blocking collectives: 73.2 us -> 134 us  [local(): totals = lax.psum(totals, name)]
  transfers between devices with their start and end apart: 8 -> 8, of which waited for: 4 -> 4; matrix products, arithmetic and copies ran while one was open for 4% -> 3% of each run, Pallas kernels for 0% -> 0%
where the time goes in v1:
time: 1890 us
  waiting for transfers between devices  991 us (52%)
  blocking collectives  664 us (35%)
  matrix products  127 us (7%)
  other arithmetic  51.7 us (3%)
  local copies, waits for them, and re-layouts  31.7 us (2%)
    psum x4, waiting for transfers between devices, local(): summed = lax.psum(partial_value, ('dom', 'kv'))  991 us
    psum x4, blocking collectives, squares(): return lax.psum(jnp.sum(residual * residual, axis=1), ('dom', 'kv'))  298 us
    psum x3, blocking collectives, local(): curvature = lax.psum(jnp.sum(direction * applied, axis=1), ('dom', 'kv'))  232 us
    psum x2, blocking collectives, local(): totals = lax.psum(totals, name)  134 us
    dot_general x4, matrix products, local(): lax.dot_general(summed * weight_pair, phase_table, (((1,), (1,)), ((), ()...  67.8 us
    dot_general x4, matrix products, local(): jnp.dot(direction, phase_table, precision=highest, preferred_element_type...  54.7 us
  transfers between devices with their start and end apart: 8, of which 4 were waited for; matrix products, arithmetic and copies ran while one was open for 3% of the time, Pallas kernels for 0%

profile of v1, /device:TPU:1, one launch (start us, length us, event | category | flops | bytes accessed | tf_op | source)
XLA Modules:
  0.0 1889.5 jit_solution(17841677040572685294)
XLA Ops:
  10.0 2.1 collective-permute-start.2
  15.6 3.1 collective-permute-start.1
  25.4 33.0 %fusion.1 = (f32[128,16384]{1,0:T(8,128)}, f32[128,16384]{1,0:T(8,128)}) fusion(f32[16384]{0:T(1024)S(1)} %bitcast.46, f32[128]{0:T(128)S(1)} %get-tuple-element.32, f32[16384]{0:T(1024)S(1)} %bitcast.47, f32[128]{0:T(128)S(1)} %get-tuple-element.33, f32[16384]{0:T(1024)S(1)} %bitcast.45, f32[128]{0:T(128)S(1)} %get-tuple-element.31), kind=kLoop, calls=%fused_computation.7 | loop fusion | flops 12582912 | bytes 16975360 | tf_op jit(solution)/shard_map/cos | solution.py:45
  58.5 10.8 gather_fusion.1
  69.3 2.1 select_bitcast_fusion
  71.5 2.8 slice_reduce_fusion.2
  75.2 3.3 fusion.3
  78.5 3.9 broadcast_multiply_fusion
  82.7 12.1 gather_fusion.3
  94.9 3.3 fusion.2
  98.2 2.2 multiply_reduce_fusion
  100.8 13.9 fusion.41
  114.8 253.6 %all-reduce.7.cloned.1.call-done = f32[2,32768]{1,0:T(2,128)} async-done(((f32[2,32768]{1,0:T(2,128)}), f32[2,32768]{1,0:T(2,128)}) %all-reduce.7.cloned.1.call-update) | async-done | bytes 262160 | tf_op jit(solution)/shard_map/psum | solution.py:175
  368.4 16.8 fusion.44
  385.2 77.9 %all-reduce.1 = (f32[2]{0:T(128)S(1)}, f32[2]{0:T(128)S(1)}) all-reduce(f32[2]{0:T(128)S(1)} %get-tuple-element.6, f32[2]{0:T(128)S(1)} %get-tuple-element.5), channel_id=1, replica_groups=mesh['dom'=64,'kv'=4] {'dom','kv'}, use_global_device_ids=true, to_apply=%region_6.7 | all-reduce | flops 4 | bytes 32 | tf_op jit(solution)/shard_map/psum | solution.py:111
  463.2 73.2 %psum.101 = f32[2]{0:T(128)S(1)} all-reduce(f32[2]{0:T(128)S(1)} %get-tuple-element.17), channel_id=1, replica_groups=mesh['dom'=64,'kv'=4] {'dom','kv'}, use_global_device_ids=true, to_apply=%region_12.13 | all-reduce | flops 2 | bytes 16 | tf_op jit(solution)/shard_map/psum | solution.py:111
  536.5 13.6 fusion.61
  550.2 245.8 %all-reduce.9.cloned.1.call-done = f32[2,32768]{1,0:T(2,128)} async-done(((f32[2,32768]{1,0:T(2,128)}), f32[2,32768]{1,0:T(2,128)}) %all-reduce.9.cloned.1.call-update) | async-done | bytes 262160 | tf_op jit(solution)/shard_map/psum | solution.py:175
  796.0 16.9 multiply_reduce_fusion.6
  812.9 77.4 %psum.103 = f32[2]{0:T(128)S(1)} all-reduce(f32[2]{0:T(128)S(1)} %get-tuple-element.37), channel_id=1, replica_groups=mesh['dom'=64,'kv'=4] {'dom','kv'}, use_global_device_ids=true, to_apply=%region_15.16 | all-reduce | flops 2 | bytes 16 | tf_op jit(solution)/shard_map/psum | solution.py:184
  890.5 73.4 %psum.104 = f32[2]{0:T(128)S(1)} all-reduce(f32[2]{0:T(128)S(1)} %get-tuple-element.15), channel_id=1, replica_groups=mesh['dom'=64,'kv'=4] {'dom','kv'}, use_global_device_ids=true, to_apply=%region_17.18 | all-reduce | flops 2 | bytes 16 | tf_op jit(solution)/shard_map/psum | solution.py:111
  964.1 13.6 fusion.60
  977.7 245.9 %all-reduce.11.cloned.1.call-done = f32[2,32768]{1,0:T(2,128)} async-done(((f32[2,32768]{1,0:T(2,128)}), f32[2,32768]{1,0:T(2,128)}) %all-reduce.11.cloned.1.call-update) | async-done | bytes 262160 | tf_op jit(solution)/shard_map/psum | solution.py:175
  1223.7 17.0 multiply_reduce_fusion.4
  1240.7 77.4 %psum.106 = f32[2]{0:T(128)S(1)} all-reduce(f32[2]{0:T(128)S(1)} %get-tuple-element.39), channel_id=1, replica_groups=mesh['dom'=64,'kv'=4] {'dom','kv'}, use_global_device_ids=true, to_apply=%region_20.21 | all-reduce | flops 2 | bytes 16 | tf_op jit(solution)/shard_map/psum | solution.py:184
  1318.3 73.5 %psum.107 = f32[2]{0:T(128)S(1)} all-reduce(f32[2]{0:T(128)S(1)} %get-tuple-element.13), channel_id=1, replica_groups=mesh['dom'=64,'kv'=4] {'dom','kv'}, use_global_device_ids=true, to_apply=%region_22.23 | all-reduce | flops 2 | bytes 16 | tf_op jit(solution)/shard_map/psum | solution.py:111
  1391.8 13.6 fusion.59
  1405.4 245.9 %all-reduce.13.cloned.1.call-done = f32[2,32768]{1,0:T(2,128)} async-done(((f32[2,32768]{1,0:T(2,128)}), f32[2,32768]{1,0:T(2,128)}) %all-reduce.13.cloned.1.call-update) | async-done | bytes 262160 | tf_op jit(solution)/shard_map/psum | solution.py:175
  1651.3 17.1 fusion.5
  1668.4 77.4 %psum.109 = f32[2]{0:T(128)S(1)} all-reduce(f32[2]{0:T(128)S(1)} %fusion.5), channel_id=1, replica_groups=mesh['dom'=64,'kv'=4] {'dom','kv'}, use_global_device_ids=true, to_apply=%region_25.26 | all-reduce | flops 2 | bytes 16 | tf_op jit(solution)/shard_map/psum | solution.py:184
  1746.0 7.8 psum.110
  1753.9 126.1 %psum.111 = f32[2]{0:T(128)S(1)} all-reduce(f32[2]{0:T(128)S(1)} %psum.110), channel_id=1, replica_groups=mesh['dom'=64,'kv'=4] {'dom'}, use_global_device_ids=true, to_apply=%region_28.29 | all-reduce | flops 2 | bytes 16 | tf_op jit(solution)/shard_map/psum | solution.py:194
  (88 shorter events, 16.7 us)
Async XLA Ops:
  7.2 93.3 %copy-start = (bf16[384,128]{1,0:T(8,128)(2,1)S(1)}, bf16[384,128]{1,0:T(8,128)(2,1)}, u32[]{:S(2)}) copy-start(bf16[384,128]{1,0:T(8,128)(2,1)} %param.24) | copy-start | bytes 294916
  7.2 361.2 %all-reduce.7.cloned.1.call-start = ((), (), s32[]{:S(2)}) async-start(), calls=%async_computation | async-start | bytes 524288 | tf_op jit(solution)/shard_map/psum | solution.py:175
  10.0 72.5 %collective-permute-start.2 = (bf16[32,128]{1,0:T(8,128)(2,1)S(1)}, bf16[32,128]{1,0:T(8,128)(2,1)S(1)}, u32[]{:S(2)}, u32[]{:S(2)}) collective-permute-start(bf16[32,128]{1,0:T(8,128)(2,1)S(1)} %get-tuple-element.29), channel_id=1, source_target_pairs={{0,1},{1,2},{2,3},{3,4},{4,5},{5,6},{6,7},{7,8},{8,9},{9,10},{10,1... | collective-permute-start | bytes 24584 | tf_op jit(solution)/shard_map/ppermute | solution.py:20
  12.1 70.4 %collective-permute-start.3 = (bf16[32,128]{1,0:T(8,128)(2,1)S(1)}, bf16[32,128]{1,0:T(8,128)(2,1)S(1)}, u32[]{:S(2)}, u32[]{:S(2)}) collective-permute-start(bf16[32,128]{1,0:T(8,128)(2,1)S(1)} %get-tuple-element.30), channel_id=1, source_target_pairs={{1,0},{2,1},{3,2},{4,3},{5,4},{6,5},{7,6},{8,7},{9,8},{10,9},{11,1... | collective-permute-start | bytes 24584 | tf_op jit(solution)/shard_map/ppermute | solution.py:23
  15.5 43.0 %collective-permute-start = (f32[32,3]{1,0:T(8,128)S(1)}, f32[32,3]{1,0:T(8,128)S(1)}, u32[]{:S(2)}, u32[]{:S(2)}) collective-permute-start(f32[32,3]{1,0:T(8,128)S(1)} %get-tuple-element.27), channel_id=1, source_target_pairs={{0,1},{1,2},{2,3},{3,4},{4,5},{5,6},{6,7},{7,8},{8,9},{9,10},{10,1... | collective-permute-start | bytes 1160 | tf_op jit(solution)/shard_map/ppermute | solution.py:20
  15.6 42.9 %collective-permute-start.1 = (f32[32,3]{1,0:T(8,128)S(1)}, f32[32,3]{1,0:T(8,128)S(1)}, u32[]{:S(2)}, u32[]{:S(2)}) collective-permute-start(f32[32,3]{1,0:T(8,128)S(1)} %get-tuple-element.28), channel_id=1, source_target_pairs={{1,0},{2,1},{3,2},{4,3},{5,4},{6,5},{7,6},{8,7},{9,8},{10,9},{11,1... | collective-permute-start | bytes 1160 | tf_op jit(solution)/shard_map/ppermute | solution.py:23
  58.4 16.8 copy-start.3
  58.4 16.8 copy-start.4
  75.2 7.4 copy-start.2
  82.7 17.8 copy-start.1
  82.7 17.8 copy-start.5
  100.8 13.9 copy-start.6
  114.7 681.3 %all-reduce.9.cloned.1.call-start = ((), (), s32[]{:S(2)}) async-start(), calls=%async_computation.1 | async-start | bytes 524288 | tf_op jit(solution)/shard_map/psum | solution.py:175
  550.1 673.5 %all-reduce.11.cloned.1.call-start = ((), (), s32[]{:S(2)}) async-start(), calls=%async_computation.2 | async-start | bytes 524288 | tf_op jit(solution)/shard_map/psum | solution.py:175
  977.7 673.6 %all-reduce.13.cloned.1.call-start = ((), (), s32[]{:S(2)}) async-start(), calls=%async_computation.3 | async-start | bytes 524288 | tf_op jit(solution)/shard_map/psum | solution.py:175
Sparse Core Ops, SparseCore 0:
  114.9 253.4 all-reduce.6
  550.2 245.7 all-reduce.8
  977.8 245.8 all-reduce.10
  1405.6 245.7 all-reduce.12
